TPU v7x, 512 devices: a whole 4x8x8 slice. The times are simulated.
512 devices in a mesh: dp: 16 (over z, core), tensor: 32 (over x, y).
Axes of the slice: x: 4, y: 8, z: 8, core: 2. Of those that a mesh axis runs over, the one named last changes fastest.
Arguments:
- activations: bfloat16 [12288, 4096], P('dp', 'tensor'), may hold values from -6 to 6
- out_grads_t: bfloat16 [5504, 12288], P('tensor', 'dp'), may hold values from -6 to 6
- in_basis: bfloat16 [4096, 4096], P(None, 'tensor'), may hold values from -0.09375 to 0.09375
- out_basis_t: bfloat16 [5504, 5504], P('tensor'), may hold values from -0.078125 to 0.078125
- query_proj: bfloat16 [4, 5504, 4096], P(None, 'tensor', 'dp'), may hold values from -6 to 6
- eigvals: float32 [5504, 4096], P('tensor', 'dp'), may hold values from 0.05 to 5
- damping: float32 [1], replicated, may hold values from 0.05 to 0.2
- lengths: int32 [96], P('dp'), may hold values from 1 to 128, 7680 in all
Outputs:
- scores: float32 [96, 4], P('dp')
Inputs may be any that keep to these rules, and one draw needn't show every extreme that they name: `lengths`: the largest token count is exactly 128.
All inputs are finite; a program needn't handle non-finite values. No bound on the sum of `lengths` on one device may be relied on, other than what follows from the above.
Results may differ from a plain program's by a relative error of at most 0.006.
Values may be sent and summed in bfloat16 or wider, within the bound.
No kernel may reach another device: no remote copies, remote signals or barrier semaphores. Data moves between devices by JAX's collectives and lax.ppermute only.
A program may use at most 128 MiB of HBM per device.

v0:
```python
import jax
import jax.numpy as jnp
from jax import lax
from jax.sharding import PartitionSpec as P


def local(activations, out_grads_t, in_basis, out_basis_t, query_proj, eigvals, damping, lengths):
    full_act = lax.all_gather(activations, "tensor", axis=1, tiled=True)
    act_local = jnp.dot(full_act, in_basis, preferred_element_type=jnp.float32).astype(jnp.bfloat16)
    act_proj = lax.all_gather(act_local, "tensor", axis=1, tiled=True)
    token_rows = full_act.shape[0]
    width = out_basis_t.shape[0]
    grad_full = jnp.dot(
        out_basis_t,
        lax.all_gather(out_grads_t, "tensor", axis=0, tiled=True),
        preferred_element_type=jnp.float32,
    )
    seq_count = lengths.shape[0]
    seq_len = token_rows // seq_count
    position = lax.broadcasted_iota(jnp.int32, (seq_count, seq_len), 1)
    keep = (position < lengths[:, None]).astype(jnp.float32).reshape(1, token_rows)
    grad_proj = (grad_full * keep).astype(jnp.bfloat16)
    scaled = (query_proj.astype(jnp.float32) / (eigvals + damping[0])).astype(jnp.bfloat16)
    projected = jnp.einsum(
        "jst,std->sjd",
        grad_proj.reshape(width, seq_count, seq_len),
        act_proj.reshape(seq_count, seq_len, act_proj.shape[1]),
        preferred_element_type=jnp.float32,
    )
    partial_value = jnp.einsum(
        "sij,qij->sq",
        projected,
        lax.all_gather(scaled, "dp", axis=2, tiled=True).astype(jnp.float32),
    )
    totals = lax.psum(partial_value, "tensor")
    norm_factor = (act_proj.shape[1] * out_basis_t.shape[1] * seq_len) ** (-0.5)
    return totals * norm_factor


def solution(mesh):
    placed = (
        P("dp", "tensor"),
        P("tensor", "dp"),
        P(None, "tensor"),
        P("tensor", None),
        P(None, "tensor", "dp"),
        P("tensor", "dp"),
        P(),
        P("dp"),
    )
    return jax.shard_map(
        local, mesh=mesh, in_specs=placed, out_specs=P("dp", None), check_vma=False
    )
```

profile of v0, /device:TPU:64, one launch (start us, length us, event | category | flops | bytes accessed | tf_op | source)
XLA Modules:
  0.0 474.7 jit_solution(10755105774203012612)
XLA Ops:
  6.5 0.0 copy-start
  6.5 0.0 copy-start.2
  6.5 0.0 copy-start.1
  6.5 0.0 copy-start.3
  6.5 0.0 all-gather.6.cloned.1.call-start
  6.6 0.7 all-gather.6.cloned.1.call-update
  7.3 0.0 all-gather.12.cloned.1.call-start
  7.3 0.7 all-gather.12.cloned.1.call-update
  8.0 0.0 all-gather.8.cloned.1.call-start
  8.1 104.2 %all-gather.6.cloned.1.call-done = bf16[768,4096]{1,0:T(8,128)(2,1)} async-done(((bf16[768,128]{1,0:T(8,128)(2,1)}), bf16[768,4096]{1,0:T(8,128)(2,1)}) %all-gather.6.cloned.1.call-update) | async-done | bytes 6291472 | tf_op jit(solution)/shard_map/all_gather | solution.py:8
  112.3 5.5 %convolution_convert_fusion = bf16[768,128]{1,0:T(8,128)(2,1)} fusion(bf16[768,4096]{1,0:T(8,128)(2,1)} %all-gather.6.cloned.1.call-done, bf16[4096,128]{1,0:T(8,128)(2,1)} %param.10), kind=kOutput, calls=%fused_computation.4 | convolution fusion | flops 805404672 | bytes 7536640 | tf_op jit(solution)/shard_map/dot_general | solution.py:9
  117.8 0.0 all-gather.8.cloned.1.call-update
  117.8 0.0 all-gather.10.cloned.1.call-start
  118.5 0.0 copy-done.2
  118.5 0.0 copy-done.1
  118.5 0.9 fusion.6
  119.5 0.0 all-gather.10.cloned.1.call-update
  119.5 0.0 copy-done.3
  119.5 0.1 convert_bitcast_fusion
  119.6 100.5 %all-gather.12.cloned.1.call-done = bf16[32,172,768]{2,1,0:T(8,128)(2,1)} async-done(((bf16[1,172,768]{2,1,0:T(8,128)(2,1)}), bf16[32,172,768]{2,1,0:T(8,128)(2,1)}) %all-gather.12.cloned.1.call-update) | async-done | bytes 8454160 | tf_op jit(solution)/shard_map/all_gather | solution.py:15
  220.1 12.5 %reshape.30 = bf16[5504,768]{1,0:T(8,128)(2,1)} reshape(bf16[32,172,768]{2,1,0:T(8,128)(2,1)} %all-gather.12.cloned.1.call-done) | data formatting | bytes 16908288
  232.6 0.0 copy-done
  232.6 5.2 %fusion.2 = bf16[172,768]{1,0:T(8,128)(2,1)S(1)} fusion(bf16[172,5504]{1,0:T(8,128)(2,1)S(1)} %copy-done, bf16[5504,768]{1,0:T(8,128)(2,1)} %reshape.30, f32[768]{0:T(1024)S(1)} %convert_bitcast_fusion), kind=kOutput, calls=%fused_computation.3 | convolution fusion | flops 1454376960 | bytes 10614784 | tf_op jit(solution)/shard_map/dot_general | solution.py:13
  237.7 0.3 reshape.26
  238.0 80.5 %all-gather.8.cloned.1.call-done = bf16[768,4096]{1,0:T(8,128)(2,1)} async-done(((bf16[768,128]{1,0:T(8,128)(2,1)}), bf16[768,4096]{1,0:T(8,128)(2,1)}) %all-gather.8.cloned.1.call-update) | async-done | bytes 6291472 | tf_op jit(solution)/shard_map/all_gather | solution.py:10
  318.6 8.5 %fusion.7 = bf16[6,172,4096]{2,1,0:T(8,128)(2,1)} fusion(bf16[6,128,4096]{2,1,0:T(8,128)(2,1)} %bitcast.14, bf16[172,6,128]{2,1,0:T(8,128)(2,1)S(1)} %reshape.26), kind=kOutput, calls=%fused_computation.8 | convolution fusion | flops 1082130432 | bytes 15009792 | tf_op jit(solution)/shard_map/jst,std->sjd/dot_general | solution.py:24
  327.1 51.2 %all-gather.10.cloned.1.call-done = bf16[4,172,4096]{2,0,1:T(4,128)(2,1)} async-done(((bf16[4,172,256]{2,0,1:T(4,128)(2,1)}), bf16[4,172,4096]{2,0,1:T(4,128)(2,1)}) %all-gather.10.cloned.1.call-update) | async-done | bytes 5636112 | tf_op jit(solution)/shard_map/all_gather | solution.py:33
  378.3 15.5 %fusion.3 = f32[6,4]{0,1:T(4,128)S(1)} fusion(bf16[4,172,4096]{2,0,1:T(4,128)(2,1)} %all-gather.10.cloned.1.call-done, bf16[6,172,4096]{2,1,0:T(8,128)(2,1)} %fusion.7), kind=kOutput, calls=%fused_computation.5 | convolution fusion | flops 33816576 | bytes 14090336 | tf_op jit(solution)/shard_map/sij,qij->sq/dot_general | solution.py:30
  393.8 73.8 %psum.7 = f32[6,4]{0,1:T(4,128)S(1)} all-reduce(f32[6,4]{0,1:T(4,128)S(1)} %fusion.3), channel_id=1, replica_groups=mesh['dp'=16,'tensor'=32] {'tensor'}, use_global_device_ids=true, to_apply=%region_0.0 | all-reduce | flops 24 | bytes 192 | tf_op jit(solution)/shard_map/psum | solution.py:35
  467.6 0.6 broadcast_multiply_fusion
  (1 shorter events, 0.0 us)
Async XLA Ops:
  6.5 226.0 %copy-start = (bf16[172,5504]{1,0:T(8,128)(2,1)S(1)}, bf16[172,5504]{1,0:T(8,128)(2,1)}, u32[]{:S(2)}) copy-start(bf16[172,5504]{1,0:T(8,128)(2,1)} %param.11) | copy-start | bytes 5680132
  6.5 111.9 %copy-start.2 = (f32[172,256]{1,0:T(8,128)S(1)}, f32[172,256]{1,0:T(8,128)}, u32[]{:S(2)}) copy-start(f32[172,256]{1,0:T(8,128)} %param.13) | copy-start | bytes 528388
  6.5 112.0 %copy-start.1 = (bf16[4,172,256]{2,0,1:T(4,128)(2,1)S(1)}, bf16[4,172,256]{2,0,1:T(4,128)(2,1)}, u32[]{:S(2)}) copy-start(bf16[4,172,256]{2,0,1:T(4,128)(2,1)} %param.12) | copy-start | bytes 1056772
  6.5 112.9 %copy-start.3 = (s32[6]{0:T(128)S(1)}, s32[6]{0:T(128)}, u32[]{:S(2)}) copy-start(s32[6]{0:T(128)} %param.15) | copy-start | bytes 76
  6.5 105.7 %all-gather.6.cloned.1.call-start = ((), (), s32[]{:S(2)}) async-start(), calls=%async_computation | async-start | bytes 6488064 | tf_op jit(solution)/shard_map/all_gather | solution.py:8
  7.3 212.8 %all-gather.12.cloned.1.call-start = ((), (), s32[]{:S(2)}) async-start(), calls=%async_computation.3 | async-start | bytes 8921088 | tf_op jit(solution)/shard_map/all_gather | solution.py:15
  8.0 310.6 %all-gather.8.cloned.1.call-start = ((), (), s32[]{:S(2)}) async-start(), calls=%async_computation.1 | async-start | bytes 6488064 | tf_op jit(solution)/shard_map/all_gather | solution.py:10
  117.8 260.5 %all-gather.10.cloned.1.call-start = ((), (), s32[]{:S(2)}) async-start(), calls=%async_computation.2 | async-start | bytes 5988352 | tf_op jit(solution)/shard_map/all_gather | solution.py:33
Sparse Core Ops, SparseCore 0:
  10.4 101.8 all-gather.5
  115.4 104.6 all-gather.11
  223.1 95.4 all-gather.7
  320.5 57.7 all-gather.9
where the time goes:
time: 475 us
  waiting for transfers between devices  338 us (71%)
  blocking collectives  73.8 us (16%)
  matrix products  34.7 us (7%)
  between operations  13.8 us (3%)
  local copies, waits for them, and re-layouts  12.8 us (3%)
    all_gather x1, waiting for transfers between devices, local(): full_act = lax.all_gather(activations, 'tensor', axis=1, tiled=True)  104 us
    all_gather x1, waiting for transfers between devices, local(): lax.all_gather(out_grads_t, 'tensor', axis=0, tiled=True)  101 us
    all_gather x1, waiting for transfers between devices, local(): act_proj = lax.all_gather(act_local, 'tensor', axis=1, tiled=True)  80.5 us
    psum x1, blocking collectives, local(): totals = lax.psum(partial_value, 'tensor')  73.8 us
    all_gather x1, waiting for transfers between devices, local(): lax.all_gather(scaled, 'dp', axis=2, tiled=True).astype(jnp.float32)  51.2 us
    dot_general x1, matrix products, local(): jnp.einsum('sij,qij->sq', projected, lax.all_gather(scaled, 'dp', axis=2,...  15.5 us
    unnamed x9, local copies, waits for them, and re-layouts  12.5 us
  transfers between devices with their start and end apart: 4, of which 4 were waited for; matrix products, arithmetic and copies ran while one was open for 7% of the time, Pallas kernels for 0%

commit v1 on v0

--- a/solution.py
+++ b/solution.py
@@ -12,7 +12,12 @@
     width = out_basis_t.shape[0]
     grad_full = jnp.dot(
         out_basis_t,
-        lax.all_gather(out_grads_t, "tensor", axis=0, tiled=True),
+        jnp.concatenate(
+            jax.lax.all_to_all(
+                jnp.stack([out_grads_t for _ in range(jax.lax.axis_size("tensor"))]), "tensor", 0, 0
+            ),
+            axis=0,
+        ),
         preferred_element_type=jnp.float32,
     )
     seq_count = lengths.shape[0]

time: 475 us -> 500 us (1.053)
  waiting for transfers between devices: 338 us -> 350 us
  starting transfers between devices: 0.15 us -> 8.24 us
    all_to_all x0 -> x1, waiting for transfers between devices: none -> 223 us  [local(): jax.lax.all_to_all(jnp.stack([out_grads_t for _ in range(jax.lax.axis_siz...]
    all_gather x1 -> x0, waiting for transfers between devices: 101 us -> none  [local(): lax.all_gather(out_grads_t, 'tensor', axis=0, tiled=True)]
    all_gather x1, waiting for transfers between devices: 80.5 us -> 0.02 us  [local(): act_proj = lax.all_gather(act_local, 'tensor', axis=1, tiled=True)]
    all_gather x1, waiting for transfers between devices: 51.2 us -> 21.5 us  [local(): lax.all_gather(scaled, 'dp', axis=2, tiled=True).astype(jnp.float32)]
    reshape x0 -> x1, local copies, waits for them, and re-layouts: none -> 12.6 us  [local(): jnp.concatenate(jax.lax.all_to_all(jnp.stack([out_grads_t for _ in range(...]
    unnamed x9 -> x10, local copies, waits for them, and re-layouts: 12.5 us -> 0.02 us
    all_to_all x0 -> x1, starting transfers between devices: none -> 8.16 us  [local(): jax.lax.all_to_all(jnp.stack([out_grads_t for _ in range(jax.lax.axis_siz...]
  transfers between devices with their start and end apart: 4 -> 4, of which waited for: 4 -> 3; matrix products, arithmetic and copies ran while one was open for 7% -> 6% of each run, Pallas kernels for 0% -> 0%
where the time goes in v1:
time: 500 us; the launch traced here: 499 us
  waiting for transfers between devices  350 us (70%)
  blocking collectives  73.8 us (15%)
  matrix products  34.8 us (7%)
  local copies, waits for them, and re-layouts  16.8 us (3%)
  between operations  13.8 us (3%)
  starting transfers between devices  8.24 us (2%)
    all_to_all x1, waiting for transfers between devices, local(): jax.lax.all_to_all(jnp.stack([out_grads_t for _ in range(jax.lax.axis_siz...  223 us
    all_gather x1, waiting for transfers between devices, local(): full_act = lax.all_gather(activations, 'tensor', axis=1, tiled=True)  105 us
    psum x1, blocking collectives, local(): totals = lax.psum(partial_value, 'tensor')  73.8 us
    all_gather x1, waiting for transfers between devices, local(): lax.all_gather(scaled, 'dp', axis=2, tiled=True).astype(jnp.float32)  21.5 us
    dot_general x1, matrix products, local(): jnp.einsum('sij,qij->sq', projected, lax.all_gather(scaled, 'dp', axis=2,...  15.5 us
    reshape x1, local copies, waits for them, and re-layouts, local(): jnp.concatenate(jax.lax.all_to_all(jnp.stack([out_grads_t for _ in range(...  12.6 us
  transfers between devices with their start and end apart: 4, of which 3 were waited for; matrix products, arithmetic and copies ran while one was open for 6% of the time, Pallas kernels for 0%

profile of v1, /device:TPU:64, one launch (start us, length us, event | category | flops | bytes accessed | tf_op | source)
XLA Modules:
  0.0 499.5 jit_solution(1430175037953232528)
XLA Ops:
  6.5 0.0 copy-start
  6.5 0.0 copy-start.2
  6.5 0.0 all-gather.4.cloned.1.call-start
  6.5 0.7 all-gather.4.cloned.1.call-update
  7.3 0.0 all-gather.6.cloned.1.call-start
  7.3 104.9 %all-gather.4.cloned.1.call-done = bf16[768,4096]{1,0:T(8,128)(2,1)} async-done(((bf16[768,128]{1,0:T(8,128)(2,1)}), bf16[768,4096]{1,0:T(8,128)(2,1)}) %all-gather.4.cloned.1.call-update) | async-done | bytes 6291472 | tf_op jit(solution)/shard_map/all_gather | solution.py:8
  112.3 5.5 %convolution_convert_fusion = bf16[768,128]{1,0:T(8,128)(2,1)} fusion(bf16[768,4096]{1,0:T(8,128)(2,1)} %all-gather.4.cloned.1.call-done, bf16[4096,128]{1,0:T(8,128)(2,1)} %param.10), kind=kOutput, calls=%fused_computation.4 | convolution fusion | flops 805404672 | bytes 7536640 | tf_op jit(solution)/shard_map/dot_general | solution.py:9
  117.8 0.0 all-gather.6.cloned.1.call-update
  117.8 0.0 copy-done.2
  117.8 3.9 stack.2
  121.7 0.0 copy-start.3
  121.7 0.0 copy-start.1
  121.7 0.0 copy-start.4
  121.7 8.2 %all-to-all-start = ((bf16[32,172,768]{2,1,0:T(8,128)(2,1)}), bf16[32,172,768]{2,1,0:T(8,128)(2,1)}, u32[]{:S(2)}, u32[]{:S(2)}) async-start(bf16[32,172,768]{2,1,0:T(8,128)(2,1)} %stack.2), calls=%async_computation | async-start | bytes 17301504 | tf_op jit(solution)/shard_map/all_to_all | solution.py:16
  129.9 0.0 all-gather.8.cloned.1.call-start
  130.6 0.0 copy-done.3
  130.6 0.0 copy-done.1
  130.6 0.9 fusion.6
  131.5 0.0 all-gather.8.cloned.1.call-update
  131.6 0.0 copy-done.4
  131.6 0.1 convert_bitcast_fusion
  131.6 223.2 %all-to-all-done = bf16[32,172,768]{2,1,0:T(8,128)(2,1)} async-done(((bf16[32,172,768]{2,1,0:T(8,128)(2,1)}), bf16[32,172,768]{2,1,0:T(8,128)(2,1)}, u32[]{:S(2)}, u32[]{:S(2)}) %all-to-all-start) | async-done | bytes 8454176 | tf_op jit(solution)/shard_map/all_to_all | solution.py:16
  354.8 12.6 %reshape.31 = bf16[5504,768]{1,0:T(8,128)(2,1)} reshape(bf16[32,172,768]{2,1,0:T(8,128)(2,1)} %all-to-all-done) | data formatting | bytes 16908288 | tf_op jit(solution)/shard_map/reshape | solution.py:15
  367.4 0.0 copy-done
  367.4 5.1 %fusion.2 = bf16[172,768]{1,0:T(8,128)(2,1)S(1)} fusion(bf16[172,5504]{1,0:T(8,128)(2,1)S(1)} %copy-done, bf16[5504,768]{1,0:T(8,128)(2,1)} %reshape.31, f32[768]{0:T(1024)S(1)} %convert_bitcast_fusion), kind=kOutput, calls=%fused_computation.3 | convolution fusion | flops 1454376960 | bytes 10614784 | tf_op jit(solution)/shard_map/dot_general | solution.py:13
  372.5 0.3 reshape.32
  372.8 0.0 all-gather.6.cloned.1.call-done
  372.8 8.7 %fusion.7 = bf16[6,172,4096]{2,1,0:T(8,128)(2,1)} fusion(bf16[6,128,4096]{2,1,0:T(8,128)(2,1)} %bitcast.13, bf16[172,6,128]{2,1,0:T(8,128)(2,1)S(1)} %reshape.32), kind=kOutput, calls=%fused_computation.8 | convolution fusion | flops 1082130432 | bytes 15009792 | tf_op jit(solution)/shard_map/jst,std->sjd/dot_general | solution.py:29
  381.5 21.5 %all-gather.8.cloned.1.call-done = bf16[4,172,4096]{2,0,1:T(4,128)(2,1)} async-done(((bf16[4,172,256]{2,0,1:T(4,128)(2,1)}), bf16[4,172,4096]{2,0,1:T(4,128)(2,1)}) %all-gather.8.cloned.1.call-update) | async-done | bytes 5636112 | tf_op jit(solution)/shard_map/all_gather | solution.py:38
  403.0 15.5 %fusion.3 = f32[6,4]{0,1:T(4,128)S(1)} fusion(bf16[4,172,4096]{2,0,1:T(4,128)(2,1)} %all-gather.8.cloned.1.call-done, bf16[6,172,4096]{2,1,0:T(8,128)(2,1)} %fusion.7), kind=kOutput, calls=%fused_computation.5 | convolution fusion | flops 33816576 | bytes 14090336 | tf_op jit(solution)/shard_map/sij,qij->sq/dot_general | solution.py:35
  418.5 73.8 %psum.7 = f32[6,4]{0,1:T(4,128)S(1)} all-reduce(f32[6,4]{0,1:T(4,128)S(1)} %fusion.3), channel_id=1, replica_groups=mesh['dp'=16,'tensor'=32] {'tensor'}, use_global_device_ids=true, to_apply=%region_0.0 | all-reduce | flops 24 | bytes 192 | tf_op jit(solution)/shard_map/psum | solution.py:40
  492.3 0.6 broadcast_multiply_fusion
  (1 shorter events, 0.0 us)
Async XLA Ops:
  6.5 360.8 %copy-start = (bf16[172,5504]{1,0:T(8,128)(2,1)S(1)}, bf16[172,5504]{1,0:T(8,128)(2,1)}, u32[]{:S(2)}) copy-start(bf16[172,5504]{1,0:T(8,128)(2,1)} %param.11) | copy-start | bytes 5680132
  6.5 111.3 %copy-start.2 = (bf16[172,768]{1,0:T(8,128)(2,1)S(1)}, bf16[172,768]{1,0:T(8,128)(2,1)}, u32[]{:S(2)}) copy-start(bf16[172,768]{1,0:T(8,128)(2,1)} %param.9) | copy-start | bytes 792580
  6.5 105.7 %all-gather.4.cloned.1.call-start = ((), (), s32[]{:S(2)}) async-start(), calls=%async_computation.1 | async-start | bytes 6488064 | tf_op jit(solution)/shard_map/all_gather | solution.py:8
  7.3 365.6 %all-gather.6.cloned.1.call-start = ((), (), s32[]{:S(2)}) async-start(), calls=%async_computation.2 | async-start | bytes 6488064 | tf_op jit(solution)/shard_map/all_gather | solution.py:10
  121.7 8.9 %copy-start.3 = (f32[172,256]{1,0:T(8,128)S(1)}, f32[172,256]{1,0:T(8,128)}, u32[]{:S(2)}) copy-start(f32[172,256]{1,0:T(8,128)} %param.13) | copy-start | bytes 528388
  121.7 8.9 %copy-start.1 = (bf16[4,172,256]{2,0,1:T(4,128)(2,1)S(1)}, bf16[4,172,256]{2,0,1:T(4,128)(2,1)}, u32[]{:S(2)}) copy-start(bf16[4,172,256]{2,0,1:T(4,128)(2,1)} %param.12) | copy-start | bytes 1056772
  121.7 9.9 %copy-start.4 = (s32[6]{0:T(128)S(1)}, s32[6]{0:T(128)}, u32[]{:S(2)}) copy-start(s32[6]{0:T(128)} %param.15) | copy-start | bytes 76
  121.7 233.1 %all-to-all-start = ((bf16[32,172,768]{2,1,0:T(8,128)(2,1)}), bf16[32,172,768]{2,1,0:T(8,128)(2,1)}, u32[]{:S(2)}, u32[]{:S(2)}) async-start(bf16[32,172,768]{2,1,0:T(8,128)(2,1)} %stack.2), calls=%async_computation | async-start | bytes 17301504 | tf_op jit(solution)/shard_map/all_to_all | solution.py:16
  129.9 273.1 %all-gather.8.cloned.1.call-start = ((), (), s32[]{:S(2)}) async-start(), calls=%async_computation.3 | async-start | bytes 5988352 | tf_op jit(solution)/shard_map/all_gather | solution.py:38
Sparse Core Ops, SparseCore 0:
  10.4 101.8 all-gather.3
  117.9 223.1 all-gather.5
  343.1 59.8 all-gather.7
